TPU v7x, 512 devices: a whole 4x8x8 slice. The times are simulated.
512 devices in a mesh: req: 128 (over y, z, core), head: 4 (over x).
Axes of the slice: x: 4, y: 8, z: 8, core: 2. Of those that a mesh axis runs over, the one named last changes fastest.
Arguments:
- queries: bfloat16 [8192, 4, 8192], P('req', None, 'head'), may hold values from -600 to 600
- new_kv: bfloat16 [8192, 4, 2, 1024], P('req', None, None, 'head'), may hold values from -6 to 6
- suffix_kv: bfloat16 [8192, 2, 32, 1024], P('req', None, None, 'head'), may hold values from -6 to 6
- prefix_kv: bfloat16 [128, 2, 512, 1024], P('req', None, None, 'head'), may hold values from -6 to 6
- prefix_id: int32 [8192, 1], P(('req', 'head')), may hold values from 0 to 127; in each aligned block of 64 rows (0 to 63, 64 to 127, ...) at most 2 rows name the same one
- suffix_len: int32 [8192], P(('req', 'head')), may hold values from 1 to 32, 131072 in all
- owner_map: int32 [128], replicated, may hold values from 0 to 127, each once
Outputs:
- attended: bfloat16 [8192, 4, 8192], P('req', None, 'head')
Inputs may be any that keep to these rules, and one draw needn't show every extreme that they name: `prefix_id`: at most 2 of the requests of one index of req name the same prefix, and in every draw some prefix is named by exactly 2 of them; popularity of prefixes is skewed. `owner_map`: each storage slot holds exactly one prefix.
All inputs are finite; a program needn't handle non-finite values. No bound on the sum of `suffix_len` on one device may be relied on, other than what follows from the above.
Results may differ from a plain program's by a relative error of at most 0.0051.
Values may be sent and summed in bfloat16 or wider, within the bound.
No kernel may reach another device: no remote copies, remote signals or barrier semaphores. Data moves between devices by JAX's collectives and lax.ppermute only.
A program may use at most 128 MiB of HBM per device.

v0:
```python
import math

import jax
import jax.numpy as jnp
from jax import lax
from jax.sharding import PartitionSpec as P

HD = 128
STEPS = 4


def prefix_live(arrived, flags, stored):
    sources, items, wide = arrived.shape
    heads_here = wide // (STEPS * HD)
    kv_heads = stored.shape[-1] // HD
    group = heads_here // kv_heads
    length = stored.shape[1]
    scale = 1.0 / HD**0.5
    total_rows = sources * items
    flat = arrived.reshape(total_rows, wide)
    live = flags.reshape(total_rows) > 0.5
    iota_rows = jnp.arange(total_rows, dtype=jnp.int32)
    order = jnp.argsort(jnp.where(live, 0, total_rows).astype(jnp.int32) + iota_rows)
    live_count = jnp.sum(live.astype(jnp.int32))
    compact = flat[order]
    block = math.gcd(total_rows, 32)
    number = (live_count + block - 1) // block
    keys = stored[0].reshape(length, kv_heads, HD)
    values = stored[1].reshape(length, kv_heads, HD)

    def one_block(index, carry):
        partial_value, largest_all, total_all = carry
        start = index * block
        query = lax.dynamic_slice_in_dim(compact, start, block, 0).reshape(
            block, STEPS, kv_heads, group, HD
        )
        score = (
            jnp.einsum("rtkgd,pkd->rtkgp", query, keys, preferred_element_type=jnp.float32) * scale
        )
        largest = jnp.max(score, axis=-1)
        weight = jnp.exp(score - largest[..., None])
        total = jnp.sum(weight, axis=-1)
        mixed = jnp.einsum(
            "rtkgp,pkd->rtkgd",
            weight.astype(jnp.bfloat16),
            values,
            preferred_element_type=jnp.float32,
        )
        mixed = (mixed / total[..., None]).astype(jnp.bfloat16)
        partial_value = lax.dynamic_update_slice_in_dim(
            partial_value, mixed.reshape(block, STEPS, heads_here * HD), start, 0
        )
        largest_all = lax.dynamic_update_slice_in_dim(
            largest_all, largest.reshape(block, STEPS, heads_here), start, 0
        )
        total_all = lax.dynamic_update_slice_in_dim(
            total_all, total.reshape(block, STEPS, heads_here), start, 0
        )
        return (partial_value, largest_all, total_all)

    start_state = (
        jnp.zeros((total_rows, STEPS, heads_here * HD), jnp.bfloat16),
        jnp.zeros((total_rows, STEPS, heads_here), jnp.float32),
        jnp.ones((total_rows, STEPS, heads_here), jnp.float32),
    )
    partial_value, largest, total = lax.fori_loop(0, number, one_block, start_state)
    partial_value = jnp.zeros_like(partial_value).at[order].set(partial_value)
    largest = jnp.zeros_like(largest).at[order].set(largest)
    total = jnp.ones_like(total).at[order].set(total)
    return (
        partial_value.reshape(sources, items, STEPS, heads_here * HD),
        largest.reshape(sources, items, STEPS, heads_here),
        total.reshape(sources, items, STEPS, heads_here),
    )


def shards(queries, new_kv, suffix_kv, prefix_kv, prefix_id, suffix_len, owner_map):
    ids_all, lengths = (
        lax.all_gather(prefix_id, "head", axis=0, tiled=True),
        lax.all_gather(suffix_len, "head", axis=0, tiled=True),
    )
    ids_here = ids_all[:, 0]
    rows = queries.shape[0]
    width = queries.shape[-1]
    heads_here = width // HD
    kv_heads = new_kv.shape[-1] // HD
    group = heads_here // kv_heads
    slots = lax.axis_size("req")
    capacity = max(2, 2 * rows // slots)
    table = owner_map.shape[0]
    scale = 1.0 / HD**0.5
    picked = ids_here[:, None] == jnp.arange(table, dtype=jnp.int32)[None, :]
    target = jnp.sum(jnp.where(picked, owner_map[None, :], 0), axis=1)
    own_store = prefix_kv[0]
    same = target[:, None] == target[None, :]
    earlier = (
        jnp.arange(rows, dtype=jnp.int32)[None, :] < jnp.arange(rows, dtype=jnp.int32)[:, None]
    )
    rank = jnp.sum(jnp.where(same & earlier, 1, 0), axis=1).astype(jnp.int32)
    place_row = target * capacity + rank
    placing = (place_row[None, :] == jnp.arange(slots * capacity, dtype=jnp.int32)[:, None]).astype(
        jnp.bfloat16
    )
    outgoing = jnp.dot(
        placing, queries.reshape(rows, STEPS * width), preferred_element_type=jnp.float32
    )
    outgoing = outgoing.astype(jnp.bfloat16).reshape(slots, capacity, STEPS * width)
    used = (
        jnp.sum(placing.astype(jnp.float32), axis=1)
        .astype(jnp.bfloat16)
        .reshape(slots, capacity, 1)
    )
    arrived = lax.all_to_all(outgoing, "req", split_axis=0, concat_axis=0, tiled=True)
    flags = lax.all_to_all(used, "req", split_axis=0, concat_axis=0, tiled=True)
    partial_value, largest, total = prefix_live(arrived, flags, own_store)
    partial_home = lax.all_to_all(partial_value, "req", split_axis=0, concat_axis=0, tiled=True)
    largest_home = lax.all_to_all(largest, "req", split_axis=0, concat_axis=0, tiled=True)
    total_home = lax.all_to_all(total, "req", split_axis=0, concat_axis=0, tiled=True)
    out_p = partial_home.reshape(slots * capacity, STEPS, width)[place_row].astype(jnp.float32)
    max_p = largest_home.reshape(slots * capacity, STEPS, heads_here)[place_row]
    sum_p = total_home.reshape(slots * capacity, STEPS, heads_here)[place_row]
    span = suffix_kv.shape[2] + STEPS
    cache_len = suffix_kv.shape[2]
    query = queries.reshape(rows, STEPS, kv_heads, group, HD)
    keys = jnp.concatenate([suffix_kv[:, 0], new_kv[:, :, 0]], axis=1).reshape(
        rows, span, kv_heads, HD
    )
    values = jnp.concatenate([suffix_kv[:, 1], new_kv[:, :, 1]], axis=1).reshape(
        rows, span, kv_heads, HD
    )
    position = jnp.arange(span, dtype=jnp.int32)
    stepidx = jnp.arange(STEPS, dtype=jnp.int32)
    live = jnp.where(
        position[None, None, :] < cache_len,
        position[None, None, :] < lengths[:, None, None],
        position[None, None, :] - cache_len <= stepidx[None, :, None],
    )
    score = jnp.einsum("rtkgd,rpkd->rtkgp", query, keys, preferred_element_type=jnp.float32) * scale
    score = jnp.where(live[:, :, None, None, :], score, -jnp.inf)
    max_s = jnp.max(score, axis=-1)
    weight = jnp.where(live[:, :, None, None, :], jnp.exp(score - max_s[..., None]), 0.0)
    sum_s = jnp.sum(weight, axis=-1)
    out_s = jnp.einsum(
        "rtkgp,rpkd->rtkgd", weight.astype(jnp.bfloat16), values, preferred_element_type=jnp.float32
    )
    out_s = (out_s / sum_s[..., None]).reshape(rows, STEPS, width)
    max_s = max_s.reshape(rows, STEPS, heads_here)
    sum_s = sum_s.reshape(rows, STEPS, heads_here)
    top = jnp.maximum(max_p, max_s)
    share_p = sum_p * jnp.exp(max_p - top)
    share_s = sum_s * jnp.exp(max_s - top)
    denom = share_p + share_s
    share_p = jnp.repeat(share_p / denom, HD, axis=-1)
    share_s = jnp.repeat(share_s / denom, HD, axis=-1)
    return (share_p * out_p + share_s * out_s).astype(jnp.bfloat16)


def solution(mesh):
    return jax.shard_map(
        shards,
        mesh=mesh,
        in_specs=(
            P("req", None, "head"),
            P("req", None, None, "head"),
            P("req", None, None, "head"),
            P("req", None, None, "head"),
            P(("req", "head"), None),
            P(("req", "head")),
            P(),
        ),
        out_specs=P("req", None, "head"),
        check_vma=False,
    )
```

profile of v0, /device:TPU:97, one launch (start us, length us, event | category | flops | bytes accessed | tf_op | source)
XLA Modules:
  0.0 480.1 jit_solution(12261935162120388880)
XLA Ops:
  3.5 6.9 %all-reduce.2 = (s32[64]{0:T(128)S(1)}, s32[64]{0:T(128)S(1)}) all-reduce(s32[64]{0:T(128)S(1)} %bitcast_dynamic-update-slice_fusion, s32[64]{0:T(128)S(1)} %dynamic-update-slice.1), channel_id=1, replica_groups=mesh['req'=128,'head'=4] {'head'}, use_global_device_ids=true, to_apply=%add | all-reduce | flops 128 | bytes 1024
  12.3 18.8 %all-to-all-start = ((bf16[128,2,1]{1,2,0:T(2,128)(2,1)}), bf16[128,2,1]{1,2,0:T(2,128)(2,1)S(1)}, u32[]{:S(2)}, u32[]{:S(2)}) async-start(bf16[128,2,1]{1,2,0:T(2,128)(2,1)} %reshape.266), calls=%async_computation | async-start | bytes 131072 | tf_op jit(solution)/shard_map/all_to_all | solution.py:114
  31.1 1.8 copy.210
  33.0 3.3 convolution_convert_fusion
  36.2 7.6 %reshape.177 = bf16[128,2,8192]{2,1,0:T(2,128)(2,1)} reshape(bf16[256,8192]{1,0:T(8,128)(2,1)} %convolution_convert_fusion) | data formatting | bytes 8388608 | tf_op jit(solution)/shard_map/reshape | solution.py:107
  43.9 15.0 %all-to-all-start.1 = ((bf16[128,2,8192]{2,1,0:T(2,128)(2,1)}), bf16[128,2,8192]{2,1,0:T(2,128)(2,1)}, u32[]{:S(2)}, u32[]{:S(2)}) async-start(bf16[128,2,8192]{2,1,0:T(2,128)(2,1)} %reshape.177), calls=%async_computation.1 | async-start | bytes 8388608 | tf_op jit(solution)/shard_map/all_to_all | solution.py:113
  61.4 3.2 sort.17
  64.5 97.4 %all-to-all-done.1 = bf16[128,2,8192]{2,1,0:T(2,128)(2,1)} async-done(((bf16[128,2,8192]{2,1,0:T(2,128)(2,1)}), bf16[128,2,8192]{2,1,0:T(2,128)(2,1)}, u32[]{:S(2)}, u32[]{:S(2)}) %all-to-all-start.1) | async-done | bytes 4194336 | tf_op jit(solution)/shard_map/all_to_all | solution.py:113
  161.9 7.2 %reshape.178 = bf16[256,8192]{1,0:T(8,128)(2,1)} reshape(bf16[128,2,8192]{2,1,0:T(2,128)(2,1)} %all-to-all-done.1) | data formatting | bytes 8388608 | tf_op jit(solution)/shard_map/reshape | solution.py:20
  169.1 11.6 %gather_fusion = bf16[256,8192]{1,0:T(8,128)(2,1)} fusion(bf16[256,8192]{1,0:T(8,128)(2,1)} %reshape.178, s32[1024]{0:T(1024)S(1)} %pad_clamp_fusion.1), kind=kCustom, calls=%fused_computation | custom fusion | bytes 8389632 | tf_op jit(solution)/shard_map/gather | solution.py:25
  180.8 4.1 broadcast.125.clone3
  184.9 22.7 %while.14 = (s32[]{:T(128)}, bf16[256,4,2048]{2,1,0:T(4,128)(2,1)}, f32[256,4,16]{0,2,1:T(8,128)S(1)}, f32[256,4,16]{0,2,1:T(8,128)S(1)}, s32[]{:T(128)}, /*inde...) while((s32[]{:T(128)}, bf16[256,4,2048]{2,1,0:T(4,128)(2,1)}, ...), condition=%wide.region_8.9_spmd, body=%wide.region_5.8_spmd.sunk | while | flops 545779712 | bytes 36282572 | solution.py:66
  186.3 2.7 bitcast_reduce_fusion.2
  189.4 3.4 fusion.56
  197.0 2.7 bitcast_reduce_fusion.2
  200.6 3.4 fusion.56
  207.9 7.1 %scatter_fusion = f32[256,4,16]{2,1,0:T(4,128)S(1)} fusion(f32[256,4,16]{2,1,0:T(4,128)S(1)} %broadcast.124, s32[256]{0:T(256)S(1)} %compare_select_fusion.1, f32[256,4,16]{2,1,0:T(4,128)S(1)} %copy.160), kind=kCustom, calls=%fused_computation.4 | custom fusion | bytes 197632 | tf_op jit(solution)/shard_map/scatter | solution.py:69
  216.6 77.1 %all-to-all-start.2 = ((f32[128,1,128]{2,1,0:T(1,128)}), f32[128,1,128]{2,1,0:T(1,128)S(1)}, u32[]{:S(2)}, u32[]{:S(2)}) async-start(f32[128,1,128]{2,1,0:T(1,128)} %reshape.282), calls=%async_computation.2 | async-start | bytes 131072 | tf_op jit(solution)/shard_map/all_to_all | solution.py:118
  294.0 7.1 %scatter_fusion.1 = f32[256,4,16]{2,1,0:T(4,128)S(1)} fusion(f32[256,4,16]{2,1,0:T(4,128)S(1)} %broadcast.126, s32[256]{0:T(256)S(1)} %compare_select_fusion.1, f32[256,4,16]{2,1,0:T(4,128)S(1)} %copy.165), kind=kCustom, calls=%fused_computation.5 | custom fusion | bytes 197632 | tf_op jit(solution)/shard_map/scatter | solution.py:68
  302.7 13.7 %all-to-all-start.3 = ((f32[128,1,128]{2,1,0:T(1,128)}), f32[128,1,128]{2,1,0:T(1,128)S(1)}, u32[]{:S(2)}, u32[]{:S(2)}) async-start(f32[128,1,128]{2,1,0:T(1,128)} %reshape.280), calls=%async_computation.3 | async-start | bytes 131072 | tf_op jit(solution)/shard_map/all_to_all | solution.py:117
  316.5 4.1 broadcast.125.clone2
  320.6 33.6 %scatter_fusion.2 = bf16[256,4,2048]{2,1,0:T(4,128)(2,1)} fusion(bf16[256,4,2048]{2,1,0:T(4,128)(2,1)} %broadcast.125.clone2, s32[256]{0:T(256)S(1)} %compare_select_fusion.1, bf16[256,4,2048]{2,1,0:T(4,128)(2,1)} %get-tuple-element.54), kind=kCustom, calls=%fused_computation.6 | custom fusion | bytes 12583936 | tf_op jit(solution)/shard_map/scatter | solution.py:67
  354.1 14.5 %all-to-all-start.4 = ((bf16[128,2,4,2048]{3,2,1,0:T(4,128)(2,1)}), bf16[128,2,4,2048]{3,2,1,0:T(4,128)(2,1)}, u32[]{:S(2)}, u32[]{:S(2)}) async-start(bf16[128,2,4,2048]{3,2,1,0:T(4,128)(2,1)} %bitcast.142), calls=%async_computation.4 | async-start | bytes 8388608 | tf_op jit(solution)/shard_map/all_to_all | solution.py:116
  373.4 1.8 slice_reduce_fusion
  377.0 2.9 fusion.19
  381.6 2.9 bitcast_divide_fusion
  384.7 1.8 reshape.269
  393.5 1.7 reshape.189
  395.8 2.0 reshape.186
  397.8 73.7 %all-to-all-done.4 = bf16[128,2,4,2048]{3,2,1,0:T(4,128)(2,1)} async-done(((bf16[128,2,4,2048]{3,2,1,0:T(4,128)(2,1)}), bf16[128,2,4,2048]{3,2,1,0:T(4,128)(2,1)}, u32[]{:S(2)}, u32[]{:S(2)}) %all-to-all-start.4) | async-done | bytes 4194336 | tf_op jit(solution)/shard_map/all_to_all | solution.py:116
  471.5 3.6 gather_fusion.3
  475.1 4.7 add_convert_fusion
  (108 shorter events, 36.4 us)
Async XLA Ops:
  12.3 31.5 %all-to-all-start = ((bf16[128,2,1]{1,2,0:T(2,128)(2,1)}), bf16[128,2,1]{1,2,0:T(2,128)(2,1)S(1)}, u32[]{:S(2)}, u32[]{:S(2)}) async-start(bf16[128,2,1]{1,2,0:T(2,128)(2,1)} %reshape.266), calls=%async_computation | async-start | bytes 131072 | tf_op jit(solution)/shard_map/all_to_all | solution.py:114
  43.9 15.0 %copy-start.5 = (bf16[1,2,512,256]{3,2,1,0:T(8,128)(2,1)S(1)}, bf16[1,2,512,256]{3,2,1,0:T(8,128)(2,1)}, u32[]{:S(2)}) copy-start(bf16[1,2,512,256]{3,2,1,0:T(8,128)(2,1)} %param.12) | copy-start | bytes 1572868
  43.9 118.1 %all-to-all-start.1 = ((bf16[128,2,8192]{2,1,0:T(2,128)(2,1)}), bf16[128,2,8192]{2,1,0:T(2,128)(2,1)}, u32[]{:S(2)}, u32[]{:S(2)}) async-start(bf16[128,2,8192]{2,1,0:T(2,128)(2,1)} %reshape.177), calls=%async_computation.1 | async-start | bytes 8388608 | tf_op jit(solution)/shard_map/all_to_all | solution.py:113
  189.4 3.5 copy-start
  200.6 3.5 copy-start
  216.6 86.1 %all-to-all-start.2 = ((f32[128,1,128]{2,1,0:T(1,128)}), f32[128,1,128]{2,1,0:T(1,128)S(1)}, u32[]{:S(2)}, u32[]{:S(2)}) async-start(f32[128,1,128]{2,1,0:T(1,128)} %reshape.282), calls=%async_computation.2 | async-start | bytes 131072 | tf_op jit(solution)/shard_map/all_to_all | solution.py:118
  302.7 51.4 %all-to-all-start.3 = ((f32[128,1,128]{2,1,0:T(1,128)}), f32[128,1,128]{2,1,0:T(1,128)S(1)}, u32[]{:S(2)}, u32[]{:S(2)}) async-start(f32[128,1,128]{2,1,0:T(1,128)} %reshape.280), calls=%async_computation.3 | async-start | bytes 131072 | tf_op jit(solution)/shard_map/all_to_all | solution.py:117
  354.1 14.5 %copy-start.2 = (bf16[64,4,2048]{2,1,0:T(4,128)(2,1)S(1)}, bf16[64,4,2048]{2,1,0:T(4,128)(2,1)}, u32[]{:S(2)}) copy-start(bf16[64,4,2048]{2,1,0:T(4,128)(2,1)} %param.9) | copy-start | bytes 3145732
  354.1 117.3 %all-to-all-start.4 = ((bf16[128,2,4,2048]{3,2,1,0:T(4,128)(2,1)}), bf16[128,2,4,2048]{3,2,1,0:T(4,128)(2,1)}, u32[]{:S(2)}, u32[]{:S(2)}) async-start(bf16[128,2,4,2048]{3,2,1,0:T(4,128)(2,1)} %bitcast.142), calls=%async_computation.4 | async-start | bytes 8388608 | tf_op jit(solution)/shard_map/all_to_all | solution.py:116
  372.4 1.0 copy-start.3
  372.8 2.5 copy-start.4
  375.3 1.0 copy-start.8
  389.0 3.6 copy-start.6
  389.0 3.6 copy-start.7
  397.8 77.4 %copy-start.1 = (f32[64,4,2048]{2,1,0:T(4,128)S(1)}, f32[64,4,2048]{2,1,0:T(4,128)}, u32[]{:S(2)}) copy-start(f32[64,4,2048]{2,1,0:T(4,128)} %reshape.269) | copy-start | bytes 6291460
where the time goes:
time: 487 us; the launch traced here: 480 us
  waiting for transfers between devices  171 us (35%)
  starting transfers between devices  139 us (29%)
  local copies, waits for them, and re-layouts  124 us (25%)
  other arithmetic  21.4 us (4%)
  matrix products  15.1 us (3%)
  blocking collectives  6.86 us (1%)
    all_to_all x1, waiting for transfers between devices, shards(): lax.all_to_all(outgoing, 'req', split_axis=0, concat_axis=0, tiled=True)  97.4 us
    all_to_all x1, starting transfers between devices, shards(): lax.all_to_all(total, 'req', split_axis=0, concat_axis=0, tiled=True)  77.1 us
    all_to_all x1, waiting for transfers between devices, shards(): lax.all_to_all(partial_value, 'req', split_axis=0, concat_axis=0, tiled=T...  73.7 us
    scatter x1, local copies, waits for them, and re-layouts, prefix_live(): partial_value = jnp.zeros_like(partial_value).at[order].set(partial_value)  33.6 us
    all_to_all x1, starting transfers between devices, shards(): flags = lax.all_to_all(used, 'req', split_axis=0, concat_axis=0, tiled=True)  18.8 us
    all_to_all x1, starting transfers between devices, shards(): lax.all_to_all(outgoing, 'req', split_axis=0, concat_axis=0, tiled=True)  15 us
    all_to_all x1, starting transfers between devices, shards(): lax.all_to_all(partial_value, 'req', split_axis=0, concat_axis=0, tiled=T...  14.5 us
    all_to_all x1, starting transfers between devices, shards(): lax.all_to_all(largest, 'req', split_axis=0, concat_axis=0, tiled=True)  13.7 us
  transfers between devices with their start and end apart: 5, of which 2 were waited for; matrix products, arithmetic and copies ran while one was open for 19% of the time, Pallas kernels for 0%

commit v1 on v0

v1 whole, which is shorter than its diff:
```python
import jax
import jax.numpy as jnp
from jax import lax
from jax.experimental import pallas as pl
from jax.experimental.pallas import tpu as pltpu
from jax.sharding import PartitionSpec as P

HD = 128
STEPS = 4
SIDE = 8
CORES = 2
GROUP = 8
QROWS = STEPS * GROUP
BATCH = 4
LOG2E = 1.4426950408889634
NT = (((1,), (1,)), ((), ()))


def device(y, z, c):
    return (y * SIDE + z) * CORES + c


ALONG_Y = [[[device(y, z, c) for y in range(SIDE)] for z in range(SIDE)] for c in range(CORES)]
ALONG_Z = [[[device(y, z, c) for z in range(SIDE)] for y in range(SIDE)] for c in range(CORES)]
ROW_GROUPS = ALONG_Y[0] + ALONG_Z[1]
EMPTY = 255


PREFIX_GROUPS = ALONG_Z[0] + ALONG_Y[1]
SWAP = [(i, i ^ 1) for i in range(SIDE * SIDE * CORES)]


def softmax_parts(score, scale):
    largest = jnp.max(score, axis=-1, keepdims=True)
    weight = jnp.exp2((score - largest) * (scale * LOG2E))
    total = jnp.sum(weight, axis=-1, keepdims=True)
    return weight, total, largest * scale


def send_kernel(source_ref, place_ref, query_ref, out_ref):
    chips, tiles = out_ref.shape[:2]
    slots = tiles - 1

    def one_chip(chip, carry):
        for i in range(slots):
            out_ref[chip, i] = query_ref[source_ref[chip * slots + i]]
        places = jnp.broadcast_to(place_ref[chip], (QROWS, HD))
        out_ref[chip, slots] = places.astype(jnp.bfloat16)
        return carry

    lax.fori_loop(0, chips, one_chip, 0)


def send(source, places, query):
    chips = places.shape[0]
    slots = source.shape[0] // chips
    return pl.pallas_call(
        send_kernel,
        out_shape=jax.ShapeDtypeStruct((chips, slots + 1) + query.shape[1:], query.dtype),
        in_specs=[pl.BlockSpec(memory_space=pltpu.SMEM)]
        + [pl.BlockSpec(memory_space=pltpu.VMEM)] * 2,
        out_specs=pl.BlockSpec(memory_space=pltpu.VMEM),
        compiler_params=pltpu.CompilerParams(vmem_limit_bytes=12 << 20),
        name="send",
    )(source, places, query)


def visit_kernel(
    note_ref, query_ref, far_ref, out_ref, kv_ref, stat, codes, places, lists, counts, batches, sems
):
    prefixes = pltpu.make_async_copy(far_ref, kv_ref, sems.at[1])
    prefixes.start()
    sources, slots = query_ref.shape[0], query_ref.shape[1] - 1
    held = kv_ref.shape[0]
    length = kv_ref.shape[1] // 2
    room = lists.shape[0] // held
    scale = 1.0 / HD**0.5
    for source in range(sources):
        row = query_ref[source, slots, :1].astype(jnp.float32)
        codes[source : source + 1] = row.astype(jnp.int32)
    to_scalars = pltpu.make_async_copy(codes, places, sems.at[0])
    to_scalars.start()
    stat[...] = jnp.zeros_like(stat)
    lane = lax.broadcasted_iota(jnp.int32, (QROWS, HD), 1)
    piece = lane // 32
    within = lane % 32
    for i in range(held):
        counts[i] = 0
    to_scalars.wait()

    def sort_source(source, filled):
        for slot in range(slots):
            place = places[source, slot]
            valid = place < held
            place = jnp.where(valid, place, 0)
            turn = counts[place]
            opens = valid & (turn % BATCH == 0)

            @pl.when(valid)
            def _(place=place, turn=turn, slot=slot):
                lists[place * room + turn] = source * slots + slot
                counts[place] = turn + 1

            @pl.when(opens)
            def _(place=place, turn=turn, filled=filled):
                batches[filled] = place * room + turn

            filled = filled + opens.astype(jnp.int32)
        return filled

    count = lax.fori_loop(0, sources, sort_source, 0)
    prefixes.wait()
    note = jnp.broadcast_to(note_ref[:1], (QROWS, HD)).astype(jnp.bfloat16)
    for source in range(sources):
        out_ref[source, slots + 1] = note

    def one_pair(pair, carry):
        work = []
        for half in range(2):
            start = batches[jnp.minimum(2 * pair + half, count - 1)]
            place = start // room
            last = place * room + counts[place] - 1
            code = [lists[jnp.minimum(start + i, last)] for i in range(BATCH)]
            work.append((place, [(c // slots, c % slots) for c in code]))
        scores = []
        for place, code in work:
            query = jnp.concatenate([query_ref[source, slot] for source, slot in code], axis=0)
            scores.append(
                lax.dot_general(
                    query, kv_ref[place, :length], NT, preferred_element_type=jnp.float32
                )
            )
        parts = [softmax_parts(score, scale) for score in scores]
        for (place, code), (weight, total, top) in zip(work, parts):
            mixed = jnp.dot(
                weight.astype(jnp.bfloat16),
                kv_ref[place, length : 2 * length],
                preferred_element_type=jnp.float32,
            )
            mixed = (mixed / total).astype(jnp.bfloat16)
            hi = top.astype(jnp.bfloat16).astype(jnp.float32)
            rest = top - hi
            mid = rest.astype(jnp.bfloat16).astype(jnp.float32)
            rest = (rest - mid) + jnp.log(total)
            low = rest.astype(jnp.bfloat16).astype(jnp.float32)
            last = rest - low
            for i, (source, slot) in enumerate(code):
                part = slice(i * QROWS, (i + 1) * QROWS)
                out_ref[source, slot] = mixed[part]
                value = jnp.where(
                    piece < 2,
                    jnp.where(piece == 0, hi[part], mid[part]),
                    jnp.where(piece == 2, low[part], last[part]),
                )
                stat[source] = jnp.where(within == slot, value, stat[source])
        return carry

    lax.fori_loop(0, (count + 1) // 2, one_pair, 0)
    out_ref[:, slots] = stat[...].astype(jnp.bfloat16)


def visit(note, query, kv):
    sources, tiles = query.shape[:2]
    held = kv.shape[0]
    room = 2 * CORES * SIDE
    return pl.pallas_call(
        visit_kernel,
        out_shape=jax.ShapeDtypeStruct((sources, tiles + 1) + query.shape[2:], query.dtype),
        in_specs=[pl.BlockSpec(memory_space=pltpu.VMEM)] * 2
        + [pl.BlockSpec(memory_space=pl.ANY)],
        out_specs=pl.BlockSpec(memory_space=pltpu.VMEM),
        scratch_shapes=[
            pltpu.VMEM(kv.shape, kv.dtype),
            pltpu.VMEM((sources, QROWS, HD), jnp.float32),
            pltpu.VMEM((sources, HD), jnp.int32),
            pltpu.SMEM((sources, HD), jnp.int32),
            pltpu.SMEM((held * room,), jnp.int32),
            pltpu.SMEM((held,), jnp.int32),
            pltpu.SMEM((held * room // BATCH,), jnp.int32),
            pltpu.SemaphoreType.DMA((2,)),
        ],
        compiler_params=pltpu.CompilerParams(vmem_limit_bytes=24 << 20),
        name="visit",
    )(note, query, kv)


def suffix_kernel(length_ref, query_ref, key_ref, value_ref, out_ref, top_ref, total_ref):
    kv_heads, rows = query_ref.shape[:2]
    span = key_ref.shape[1]
    cache = span - 16
    scale = 1.0 / HD**0.5
    base = pl.program_id(0) * rows
    slot = lax.broadcasted_iota(jnp.int32, (QROWS, span), 1)
    step = lax.broadcasted_iota(jnp.int32, (QROWS, span), 0) // GROUP
    fresh = (slot >= cache) & (slot - cache <= step)
    cols = [slice(k * HD, (k + 1) * HD) for k in range(kv_heads)]
    items = [(k, r) for r in range(rows) for k in range(kv_heads)]
    scores = []
    for k, r in items:
        score = lax.dot_general(
            query_ref[k, r], key_ref[r, :, cols[k]], NT, preferred_element_type=jnp.float32
        )
        live = fresh | (slot < jnp.minimum(length_ref[base + r], cache))
        scores.append(jnp.where(live, score, -jnp.inf))
    weight, total, top = softmax_parts(jnp.concatenate(scores, axis=0), scale)
    weight = weight.astype(jnp.bfloat16)
    mixed = [
        jnp.dot(
            weight[i * QROWS : (i + 1) * QROWS],
            value_ref[r, :, cols[k]],
            preferred_element_type=jnp.float32,
        )
        for i, (k, r) in enumerate(items)
    ]
    top = jnp.broadcast_to(top, (len(items) * QROWS, HD))
    total = jnp.broadcast_to(total, (len(items) * QROWS, HD))
    for i, (k, r) in enumerate(items):
        part = slice(i * QROWS, (i + 1) * QROWS)
        out_ref[k, r] = mixed[i]
        top_ref[k, r] = top[part]
        total_ref[k, r] = total[part]


def suffix(lengths, query, keys, values):
    kv_heads, rows = query.shape[:2]
    chunk = 8
    span = keys.shape[1]
    by_row = pl.BlockSpec((kv_heads, chunk, QROWS, HD), lambda i, n: (0, i, 0, 0))
    by_slot = pl.BlockSpec((chunk, span, kv_heads * HD), lambda i, n: (i, 0, 0))
    return pl.pallas_call(
        suffix_kernel,
        out_shape=(jax.ShapeDtypeStruct((kv_heads, rows, QROWS, HD), jnp.float32),) * 3,
        grid_spec=pltpu.PrefetchScalarGridSpec(
            num_scalar_prefetch=1,
            grid=(rows // chunk,),
            in_specs=[by_row, by_slot, by_slot],
            out_specs=(by_row,) * 3,
        ),
        compiler_params=pltpu.CompilerParams(vmem_limit_bytes=16 << 20),
        cost_estimate=pl.CostEstimate(
            flops=4 * rows * kv_heads * QROWS * span * HD,
            bytes_accessed=8 << 20,
            transcendentals=rows * kv_heads * QROWS * span,
        ),
        name="suffix",
    )(lengths, query, keys, values)


def join_kernel(
    core_ref, table_ref, mine_ref, theirs_ref, suf_ref, top_ref, total_ref, out_ref
):
    rows = suf_ref.shape[1]
    for which, block in enumerate((mine_ref, theirs_ref)):
        head = which ^ core_ref[0]

        def one_row(r, carry, block=block, which=which, head=head):
            far = block[table_ref[(3 * which + 1) * rows + r]].astype(jnp.float32)
            far = far + pltpu.roll(far, HD - 32, 1)
            lane = table_ref[(3 * which + 2) * rows + r]
            max_p = jnp.take_along_axis(far, jnp.full(far.shape, lane, jnp.int32), axis=1)
            log_p = jnp.take_along_axis(far, jnp.full(far.shape, lane + 64, jnp.int32), axis=1)
            max_s = top_ref[head, r]
            top = jnp.maximum(max_p, max_s)
            share_p = jnp.exp((max_p - top) + log_p)
            scale_s = jnp.exp(max_s - top)
            value = block[table_ref[3 * which * rows + r]].astype(jnp.float32)
            mixed = share_p * value + scale_s * suf_ref[head, r]
            whole = share_p + scale_s * total_ref[head, r]
            out_ref[head, r] = (mixed / whole).astype(jnp.bfloat16)
            return carry

        lax.fori_loop(0, rows, one_row, 0, unroll=8)


def join(core, table, mine, theirs, near):
    kv_heads, rows = near[0].shape[:2]
    return pl.pallas_call(
        join_kernel,
        out_shape=jax.ShapeDtypeStruct((kv_heads, rows, QROWS, HD), jnp.bfloat16),
        in_specs=[pl.BlockSpec(memory_space=pltpu.SMEM)] * 2
        + [pl.BlockSpec(memory_space=pltpu.VMEM)] * 5,
        out_specs=pl.BlockSpec(memory_space=pltpu.VMEM),
        compiler_params=pltpu.CompilerParams(vmem_limit_bytes=24 << 20),
        name="join",
    )(core, table, mine, theirs, *near)


def shards(queries, new_kv, suffix_kv, prefix_kv, prefix_id, suffix_len, owner_map):
    rows, _, width = queries.shape
    kv_heads = new_kv.shape[-1] // HD
    me = lax.axis_index("req")
    core = me % CORES

    def swap(array):
        return lax.ppermute(array, "req", SWAP)

    stored = prefix_kv[0].reshape(-1, kv_heads, HD)
    mine, other = stored[:, 0], stored[:, 1]
    mine, other = jnp.where(core == 0, mine, other), jnp.where(core == 0, other, mine)
    mine, other, prefix_id = lax.optimization_barrier((mine, other, prefix_id))
    kv = lax.all_gather(
        jnp.stack([mine, swap(other)]),
        "req",
        axis_index_groups=PREFIX_GROUPS,
        axis=0,
        tiled=True,
    )

    heads = lax.axis_size("head")
    chip_size = heads * CORES
    chips = [[c * chip_size + i for i in range(chip_size)] for c in range(SIDE * SIDE)]
    meta = jnp.stack([prefix_id[:, 0], suffix_len])
    position = core * heads + lax.axis_index("head")
    spot = jnp.arange(chip_size, dtype=jnp.int32)[:, None, None] == position
    meta = lax.psum(jnp.where(spot, meta, 0), ("req", "head"), axis_index_groups=chips)
    ids = meta[:, 0].reshape(CORES, rows)
    lengths = lax.dynamic_index_in_dim(meta[:, 1].reshape(CORES, rows), core, 0, keepdims=False)
    ids = jnp.where(core == 0, ids, ids[::-1])
    table = owner_map.shape[0]
    picked = ids[..., None] == jnp.arange(table, dtype=jnp.int32)
    slot = jnp.sum(jnp.where(picked, owner_map, 0), axis=-1)

    def coordinate(slot, along_y):
        return jnp.where(along_y, slot // (CORES * SIDE), (slot // CORES) % SIDE)

    row = jnp.arange(rows, dtype=jnp.int32)
    before = row[None, :] < row[:, None]

    def rank_of(goal):
        same = goal[..., None, :] == goal[..., :, None]
        return jnp.sum(jnp.where(same & before, 1, 0), axis=-1)

    capacity = rows // 4
    rounds = 2
    slots = CORES * capacity
    wide, narrow = slots + 2, capacity + 1
    goal, cross_goal = coordinate(slot, core == 0), coordinate(slot, core != 0)
    rank, cross_rank = rank_of(goal), rank_of(cross_goal)
    fullest = 1 + jnp.maximum(jnp.max(rank), jnp.max(cross_rank))
    place = cross_goal * CORES + jnp.where(slot % CORES == core, 0, 1)

    query = queries.reshape(rows, STEPS, kv_heads, GROUP, HD)
    query = jnp.transpose(query, (2, 0, 1, 3, 4)).reshape(kv_heads, rows, QROWS, HD)
    own_rows = lax.dynamic_index_in_dim(query, core, 0, keepdims=False)
    other_rows = swap(lax.dynamic_index_in_dim(query, 1 - core, 0, keepdims=False))
    both = jnp.concatenate([own_rows, other_rows])

    def pack(turn):
        chip = jnp.arange(SIDE, dtype=jnp.int32)[:, None, None, None]
        spot = turn * capacity + jnp.arange(capacity, dtype=jnp.int32)[:, None]
        sent = (goal[:, None, :] == chip) & (rank[:, None, :] == spot)
        index = jnp.arange(CORES * rows, dtype=jnp.int32).reshape(CORES, 1, rows)
        from_row = jnp.sum(jnp.where(sent, index, 0), axis=-1).reshape(-1)
        places = EMPTY + jnp.sum(jnp.where(sent, place[:, None, :] - EMPTY, 0), axis=-1)
        places = places.astype(jnp.float32).reshape(SIDE, 1, slots)
        places = jnp.pad(places, ((0, 0), (0, 0), (0, HD - slots)), constant_values=EMPTY)
        at_end = jnp.arange(HD, dtype=jnp.int32) == HD - 1
        places = jnp.where(at_end, fullest.astype(jnp.float32), places)
        return send(from_row, places, both)

    def trade(blocks):
        return lax.all_to_all(blocks, "req", 0, 0, axis_index_groups=ROW_GROUPS, tiled=True)

    outgoing = pack(0)
    outgoing, lengths = lax.optimization_barrier((outgoing, lengths))
    arrived = trade(outgoing)
    pad = jnp.zeros((rows, 16 - STEPS, kv_heads * HD), jnp.bfloat16)
    keys = jnp.concatenate([suffix_kv[:, 0], new_kv[:, :, 0], pad], axis=1)
    values = jnp.concatenate([suffix_kv[:, 1], new_kv[:, :, 1], pad], axis=1)
    near = suffix(lengths, query, keys, values)
    arrived, near = lax.optimization_barrier((arrived, near))
    note = jnp.max(arrived[:, slots, 0, HD - 1].astype(jnp.float32))
    note = jnp.broadcast_to(note, (8, HD))
    note = jnp.maximum(note, swap(note))

    def come_home(done):
        back = trade(done)
        theirs = swap(back[:, capacity : slots + 1])
        fullest = jnp.max(back[:, slots + 1, 0].astype(jnp.float32))
        return back.reshape(-1, QROWS, HD), theirs.reshape(-1, QROWS, HD), fullest

    cross_goal, cross_rank = cross_goal[0], cross_rank[0]
    turn, cross_turn = rank[0] // capacity, cross_rank // capacity
    at, cross_at = rank[0] % capacity, cross_rank % capacity
    base = (turn * SIDE + goal[0]) * wide
    cross_base = (cross_turn * SIDE + cross_goal) * narrow
    home = jnp.stack(
        [
            base + at,
            base + slots,
            at,
            cross_base + cross_at,
            cross_base + capacity,
            capacity + cross_at,
        ]
    ).reshape(-1)
    which = core.reshape(1).astype(jnp.int32)
    arrived, home = lax.optimization_barrier((arrived, home))
    back, theirs, fullest = come_home(visit(note, arrived, kv))

    def finish(back, theirs, both, note, kv, near):
        return join(which, home, back, theirs, near)

    def finish_rest(back, theirs, both, note, kv, near):
        backs, others = [back], [theirs]
        for turn in range(1, rounds):
            done = visit(note, trade(pack(turn)), kv)
            more = come_home(done)
            backs.append(more[0])
            others.append(more[1])
        return join(which, home, jnp.concatenate(backs), jnp.concatenate(others), near)

    out = lax.cond(fullest <= capacity, finish, finish_rest, back, theirs, both, note, kv, near)
    out = out.reshape(kv_heads, rows, STEPS, GROUP, HD)
    return jnp.transpose(out, (1, 2, 0, 3, 4)).reshape(rows, STEPS, width)


def solution(mesh):
    return jax.shard_map(
        shards,
        mesh=mesh,
        in_specs=(
            P("req", None, "head"),
            P("req", None, None, "head"),
            P("req", None, None, "head"),
            P("req", None, None, "head"),
            P(("req", "head"), None),
            P(("req", "head")),
            P(),
        ),
        out_specs=P("req", None, "head"),
        check_vma=False,
    )
```

time: 487 us -> 166 us (0.34)
  the two profiles are of different devices: /device:TPU:97 before, /device:TPU:1 now
where the time goes in v1:
time: 166 us; the launch traced here: 164 us
  blocking collectives  45.3 us (27%)
  waiting for transfers between devices  32.2 us (19%)
  Pallas kernels  25.2 us (15%)
  starting transfers between devices  23.8 us (14%)
  between operations  17 us (10%)
  local copies, waits for them, and re-layouts  11.3 us (7%)
  other arithmetic  9.4 us (6%)
    all_to_all x1, blocking collectives, trade(): lax.all_to_all(blocks, 'req', 0, 0, axis_index_groups=ROW_GROUPS, tiled=T...  38.3 us
    all_to_all x1, waiting for transfers between devices, trade(): lax.all_to_all(blocks, 'req', 0, 0, axis_index_groups=ROW_GROUPS, tiled=T...  31 us
    ppermute x4, starting transfers between devices, swap(): return lax.ppermute(array, 'req', SWAP)  15.8 us
    pallas_call x1, Pallas kernels, visit(): pl.pallas_call(visit_kernel, out_shape=jax.ShapeDtypeStruct((sources, til...  10.4 us
    all_to_all x1, starting transfers between devices, trade(): lax.all_to_all(blocks, 'req', 0, 0, axis_index_groups=ROW_GROUPS, tiled=T...  7.99 us
    pallas_call x1, Pallas kernels, join(): pl.pallas_call(join_kernel, out_shape=jax.ShapeDtypeStruct((kv_heads, row...  7.55 us
    psum x1, blocking collectives, shards(): lax.psum(jnp.where(spot, meta, 0), ('req', 'head'), axis_index_groups=chips)  7 us
    pallas_call x1, Pallas kernels, suffix(): pl.pallas_call(suffix_kernel, out_shape=(jax.ShapeDtypeStruct((kv_heads,...  6.43 us
  transfers between devices with their start and end apart: 6, of which 3 were waited for; matrix products, arithmetic and copies ran while one was open for 8% of the time, Pallas kernels for 4%

profile of v1, /device:TPU:1, one launch (start us, length us, event | category | flops | bytes accessed | tf_op | source)
XLA Modules:
  0.0 164.3 jit_solution(11056376098977981471)
XLA Ops:
  6.5 1.3 reshape_squeeze.9
  7.8 1.2 broadcast_select_fusion.1
  9.1 0.7 copy.63
  9.8 8.8 %collective-permute-start.3 = (bf16[1024,128]{1,0:T(8,128)(2,1)}, bf16[1024,128]{1,0:T(8,128)(2,1)}, u32[]{:S(2)}, u32[]{:S(2)}) collective-permute-start(bf16[1024,128]{1,0:T(8,128)(2,1)} %bitcast.49), channel_id=1, source_target_pairs={{0,4},{4,0},{8,12},{12,8},{16,20},{20,16},{24,28},{28,24},{32,36},... | collective-permute-start | bytes 786440 | tf_op jit(solution)/shard_map/ppermute | solution.py:295
  18.6 0.7 reshape.286
  19.7 1.9 %collective-permute-start.1 = (bf16[64,32,128]{2,1,0:T(8,128)(2,1)S(1)}, bf16[64,32,128]{2,1,0:T(8,128)(2,1)S(1)}, u32[]{:S(2)}, u32[]{:S(2)}) collective-permute-start(bf16[64,32,128]{2,1,0:T(8,128)(2,1)S(1)} %get-tuple-element.124), channel_id=1, source_target_pairs={{0,4},{4,0},{8,12},{12,8},{16,20},{20,16},{24,28},{28,24},{32,36},... | collective-permute-start | bytes 1572872 | tf_op jit(solution)/shard_map/ppermute | solution.py:295
  21.6 1.8 %pad_maximum_fusion.3 = bf16[2,1024,128]{2,1,0:T(8,128)(2,1)} fusion(bf16[1,1024,128]{2,1,0:T(8,128)(2,1)} %bitcast.15, bf16[1,1024,128]{2,1,0:T(8,128)(2,1)S(1)} %bitcast.57), kind=kLoop, calls=%fused_computation.23 | loop fusion | flops 262144 | bytes 1048576 | tf_op jit(solution)/shard_map/stack | solution.py:302
  23.6 7.0 %psum.7 = s32[8,2,16]{2,0,1:T(8,128)S(1)} all-reduce(s32[8,2,16]{2,0,1:T(8,128)S(1)} %broadcast_select_fusion.4), channel_id=1, replica_groups={{0,1,2,3,4,5,6,7},{8,9,10,11,12,13,14,15},{16,17,18,19,20,21,22,23},{24..., use_global_device_ids=true, to_apply=%region_0.1 | all-reduce | flops 256 | bytes 2048 | tf_op jit(solution)/shard_map/psum | solution.py:315
  31.2 0.6 fusion.3
  32.1 0.6 reduce_max.46
  32.7 0.6 reduce_max.47
  34.8 0.8 copy-done.9
  35.5 1.1 pad_maximum_fusion.2.query_ref
  36.7 0.9 send.3
  37.6 1.4 copy-done
  39.0 8.0 %all-to-all-start.2 = ((bf16[8,33,32,128]{3,2,1,0:T(8,128)(2,1)}), bf16[8,33,32,128]{3,2,1,0:T(8,128)(2,1)S(1)}, u32[]{:S(2)}, u32[]{:S(2)}) async-start(bf16[8,33,32,128]{3,2,1,0:T(8,128)(2,1)} %copy-done), calls=%async_computation.2 | async-start | bytes 4325376 | tf_op jit(solution)/shard_map/all_to_all | solution.py:362
  47.6 1.8 %slice_bitcast_fusion = (bf16[64,32,256]{2,1,0:T(8,128)(2,1)S(1)}, bf16[64,32,256]{2,1,0:T(8,128)(2,1)S(1)}) fusion(bf16[64,2,32,256]{3,2,1,0:T(8,128)(2,1)} %param.11), kind=kLoop, calls=%fused_computation.19 | loop fusion | bytes 4194304 | tf_op jit(solution)/shard_map/squeeze | solution.py:369
  49.4 1.3 maximum_maximum_fusion.1
  50.6 6.4 %suffix.1 = (f32[2,64,32,128]{3,2,1,0:T(8,128)}, f32[2,64,32,128]{3,2,1,0:T(8,128)}, f32[2,64,32,128]{3,2,1,0:T(8,128)}) custom-call(s32[64]{0:T(128)S(1)} %fusion.6.length_ref, bf16[2,64,32,128]{3,2,1,0:T(8,128)(2,1)S(1)} %bitcast.52, bf16[64,48,256]{2,1,0:T(8,128)(2,1)S(1)} %get-tuple-element.132.key_ref, bf16[64,48,256]{2,1,0:T(8,128)(2,1)S(1)} %get-tuple-element.131.value_ref), custom_call_target="tpu_custom_call" | custom-call | flops 100663296 | bytes 8388608 | tf_op jit(solution)/shard_map/suffix/pallas_call | solution.py:230
  57.1 31.0 %all-to-all-done.2.query_ref = bf16[8,33,32,128]{3,2,1,0:T(8,128)(2,1)S(1)} async-done(((bf16[8,33,32,128]{3,2,1,0:T(8,128)(2,1)}), bf16[8,33,32,128]{3,2,1,0:T(8,128)(2,1)S(1)}, u32[]{:S(2)}, u32[]{:S(2)}) %all-to-all-start.2) | async-done | bytes 2162720 | tf_op jit(solution)/shard_map/all_to_all | solution.py:362
  88.1 0.7 slice_reduce_fusion.1
  88.8 0.7 broadcast_in_dim.125
  89.5 1.9 %collective-permute-start.2 = (f32[8,128]{1,0:T(8,128)S(1)}, f32[8,128]{1,0:T(8,128)S(1)}, u32[]{:S(2)}, u32[]{:S(2)}) collective-permute-start(f32[8,128]{1,0:T(8,128)S(1)} %broadcast_in_dim.125), channel_id=1, source_target_pairs={{0,4},{4,0},{8,12},{12,8},{16,20},{20,16},{24,28},{28,24},{32,36},... | collective-permute-start | bytes 12296 | tf_op jit(solution)/shard_map/ppermute | solution.py:295
  92.6 10.4 %visit.3 = bf16[8,34,32,128]{3,2,1,0:T(8,128)(2,1)S(1)} custom-call(f32[8,128]{1,0:T(8,128)S(1)} %broadcast_maximum_fusion.note_ref, bf16[8,33,32,128]{3,2,1,0:T(8,128)(2,1)S(1)} %all-to-all-done.2.query_ref, bf16[16,1024,128]{2,1,0:T(8,128)(2,1)} %all-gather.2.cloned.1.call-done.far_ref), custom_call_target="tpu_custom_call" | custom-call | tf_op jit(solution)/shard_map/visit/pallas_call | solution.py:166
  103.0 38.3 %all_to_all.20 = bf16[8,34,32,128]{3,2,1,0:T(8,128)(2,1)S(1)} all-to-all(bf16[8,34,32,128]{3,2,1,0:T(8,128)(2,1)S(1)} %visit.3), channel_id=1, replica_groups={{0,64,128,192,256,320,384,448},{8,72,136,200,264,328,392,456},{16,80,14..., dimensions={0} | all-to-all | bytes 4456448 | tf_op jit(solution)/shard_map/all_to_all | solution.py:362
  141.3 1.2 slice.70
  142.5 3.2 %collective-permute-start.4 = (bf16[8,17,32,128]{3,2,1,0:T(8,128)(2,1)}, bf16[8,17,32,128]{3,2,1,0:T(8,128)(2,1)}, u32[]{:S(2)}, u32[]{:S(2)}) collective-permute-start(bf16[8,17,32,128]{3,2,1,0:T(8,128)(2,1)} %slice.70), channel_id=1, source_target_pairs={{0,4},{4,0},{8,12},{12,8},{16,20},{20,16},{24,28},{28,24},{32,36},... | collective-permute-start | bytes 3342344 | tf_op jit(solution)/shard_map/ppermute | solution.py:295
  145.8 0.7 slice_reduce_fusion
  147.7 0.8 collective-permute-done.4
  148.5 7.5 %conditional.1 = (bf16[2,64,32,128]{3,2,1,0:T(8,128)(2,1)S(1)}) conditional(s32[]{:T(128)} %convert_element_type.40, (s32[2,64]{1,0:T(2,128)S(1)}, s32[2,64]{1,0:T(2,128)S(1)}, f32[]{:T(128)}, s32[2,64]{1,0:T(2,128)S(1)}, bf16[128,32,128]{2,1,0:T(8,128)(2,1)S(1)}, /*index=5*/f32[8,128]{1,0:T(8,128)S(1)}, bf16[16,1024,128]{2,1,0:T(8,128)(2,1)}, ...), branch_computations={%region_10.13_spmd, %region_13.14_spmd} | conditional | flops 3428880 | bytes 70802464 | solution.py:413
  148.5 7.5 %join.3 = bf16[2,64,32,128]{3,2,1,0:T(8,128)(2,1)S(1)} custom-call(s32[1]{0:T(128)} %get-tuple-element.64.core_ref, s32[384]{0:T(512)S(1)} %get-tuple-element.65.table_ref, bf16[272,32,128]{2,1,0:T(8,128)(2,1)S(1)} %get-tuple-element.66.mine_ref, bf16[136,32,128]{2,1,0:T(8,128)(2,1)} %get-tuple-element.67.theirs_ref, ...), custom_call_target="tpu_custom_call" | custom-call | tf_op jit(solution)/shard_map/cond/branch_1_fun/join/pallas_call | solution.py:277
  156.3 1.1 reshape.293
  (59 shorter events, 2.7 us)
Async XLA Ops:
  6.5 86.1 %all-gather.2.cloned.1.call-start = ((), (), s32[]{:S(2)}) async-start(), calls=%async_computation.4 | async-start | bytes 4718592 | tf_op jit(solution)/shard_map/all_gather | solution.py:301
  6.5 12.1 %copy-start.7 = (bf16[64,4,2048]{2,1,0:T(4,128)(2,1)S(1)}, bf16[64,4,2048]{2,1,0:T(4,128)(2,1)}, u32[]{:S(2)}) copy-start(bf16[64,4,2048]{2,1,0:T(4,128)(2,1)} %param.9) | copy-start | bytes 3145732
  9.8 11.8 %collective-permute-start.3 = (bf16[1024,128]{1,0:T(8,128)(2,1)}, bf16[1024,128]{1,0:T(8,128)(2,1)}, u32[]{:S(2)}, u32[]{:S(2)}) collective-permute-start(bf16[1024,128]{1,0:T(8,128)(2,1)} %bitcast.49), channel_id=1, source_target_pairs={{0,4},{4,0},{8,12},{12,8},{16,20},{20,16},{24,28},{28,24},{32,36},... | collective-permute-start | bytes 786440 | tf_op jit(solution)/shard_map/ppermute | solution.py:295
  19.3 2.3 %copy-start.11 = (s32[16]{0:T(128)S(1)}, s32[16]{0:T(128)}, u32[]{:S(2)}) copy-start(s32[16]{0:T(128)} %param.14) | copy-start | bytes 196
  19.3 2.3 %copy-start.12 = (s32[16,1]{0,1:T(1,128)S(1)}, s32[16,1]{0,1:T(1,128)}, u32[]{:S(2)}) copy-start(s32[16,1]{0,1:T(1,128)} %param.13) | copy-start | bytes 196
  19.5 11.2 %copy-start.10 = (s32[128]{0:T(128)S(1)}, s32[128]{0:T(128)}, u32[]{:S(2)}) copy-start(s32[128]{0:T(128)} %param.15) | copy-start | bytes 1540
  19.7 15.1 %collective-permute-start.1 = (bf16[64,32,128]{2,1,0:T(8,128)(2,1)S(1)}, bf16[64,32,128]{2,1,0:T(8,128)(2,1)S(1)}, u32[]{:S(2)}, u32[]{:S(2)}) collective-permute-start(bf16[64,32,128]{2,1,0:T(8,128)(2,1)S(1)} %get-tuple-element.124), channel_id=1, source_target_pairs={{0,4},{4,0},{8,12},{12,8},{16,20},{20,16},{24,28},{28,24},{32,36},... | collective-permute-start | bytes 1572872 | tf_op jit(solution)/shard_map/ppermute | solution.py:295
  34.7 0.8 copy-start.9
  36.7 2.3 %copy-start.2 = (bf16[128,32,128]{2,1,0:T(8,128)(2,1)}, bf16[128,32,128]{2,1,0:T(8,128)(2,1)S(1)}, u32[]{:S(2)}) copy-start(bf16[128,32,128]{2,1,0:T(8,128)(2,1)S(1)} %pad_maximum_fusion.2.query_ref) | copy-start | bytes 3145732
  37.6 1.4 copy-start
  39.0 8.1 %copy-start.8 = (bf16[64,4,2,256]{3,2,1,0:T(2,128)(2,1)S(1)}, bf16[64,4,2,256]{3,2,1,0:T(2,128)(2,1)}, u32[]{:S(2)}) copy-start(bf16[64,4,2,256]{3,2,1,0:T(2,128)(2,1)} %param.10) | copy-start | bytes 786436
  39.0 49.1 %all-to-all-start.2 = ((bf16[8,33,32,128]{3,2,1,0:T(8,128)(2,1)}), bf16[8,33,32,128]{3,2,1,0:T(8,128)(2,1)S(1)}, u32[]{:S(2)}, u32[]{:S(2)}) async-start(bf16[8,33,32,128]{3,2,1,0:T(8,128)(2,1)} %copy-done), calls=%async_computation.2 | async-start | bytes 4325376 | tf_op jit(solution)/shard_map/all_to_all | solution.py:362
  89.5 3.1 %collective-permute-start.2 = (f32[8,128]{1,0:T(8,128)S(1)}, f32[8,128]{1,0:T(8,128)S(1)}, u32[]{:S(2)}, u32[]{:S(2)}) collective-permute-start(f32[8,128]{1,0:T(8,128)S(1)} %broadcast_in_dim.125), channel_id=1, source_target_pairs={{0,4},{4,0},{8,12},{12,8},{16,20},{20,16},{24,28},{28,24},{32,36},... | collective-permute-start | bytes 12296 | tf_op jit(solution)/shard_map/ppermute | solution.py:295
  141.3 7.2 %copy-start.3 = (bf16[128,32,128]{2,1,0:T(8,128)(2,1)S(1)}, bf16[128,32,128]{2,1,0:T(8,128)(2,1)}, u32[]{:S(2)}) copy-start(bf16[128,32,128]{2,1,0:T(8,128)(2,1)} %copy-done.2) | copy-start | bytes 3145732
  142.5 5.9 %collective-permute-start.4 = (bf16[8,17,32,128]{3,2,1,0:T(8,128)(2,1)}, bf16[8,17,32,128]{3,2,1,0:T(8,128)(2,1)}, u32[]{:S(2)}, u32[]{:S(2)}) collective-permute-start(bf16[8,17,32,128]{3,2,1,0:T(8,128)(2,1)} %slice.70), channel_id=1, source_target_pairs={{0,4},{4,0},{8,12},{12,8},{16,20},{20,16},{24,28},{28,24},{32,36},... | collective-permute-start | bytes 3342344 | tf_op jit(solution)/shard_map/ppermute | solution.py:295
Sparse Core Ops, SparseCore 0:
  23.6 61.3 all-gather.1

commit v2 on v1

--- a/solution.py
+++ b/solution.py
@@ -298,13 +298,7 @@
     mine, other = stored[:, 0], stored[:, 1]
     mine, other = jnp.where(core == 0, mine, other), jnp.where(core == 0, other, mine)
     mine, other, prefix_id = lax.optimization_barrier((mine, other, prefix_id))
-    kv = lax.all_gather(
-        jnp.stack([mine, swap(other)]),
-        "req",
-        axis_index_groups=PREFIX_GROUPS,
-        axis=0,
-        tiled=True,
-    )
+    other = swap(other)
 
     heads = lax.axis_size("head")
     chip_size = heads * CORES
@@ -313,6 +307,10 @@
     position = core * heads + lax.axis_index("head")
     spot = jnp.arange(chip_size, dtype=jnp.int32)[:, None, None] == position
     meta = lax.psum(jnp.where(spot, meta, 0), ("req", "head"), axis_index_groups=chips)
+    meta, mine, other = lax.optimization_barrier((meta, mine, other))
+    kv = lax.all_gather(
+        jnp.stack([mine, other]), "req", axis_index_groups=PREFIX_GROUPS, axis=0, tiled=True
+    )
     ids = meta[:, 0].reshape(CORES, rows)
     lengths = lax.dynamic_index_in_dim(meta[:, 1].reshape(CORES, rows), core, 0, keepdims=False)
     ids = jnp.where(core == 0, ids, ids[::-1])

time: 166 us -> 165 us (level)
  blocking collectives: 45.3 us -> 50.1 us
  waiting for transfers between devices: 32.2 us -> 29.7 us
    all_to_all x1, blocking collectives: 38.3 us -> 43.6 us  [trade(): lax.all_to_all(blocks, 'req', 0, 0, axis_index_groups=ROW_GROUPS, tiled=T...]
    all_to_all x1, waiting for transfers between devices: 31 us -> 28.5 us  [trade(): lax.all_to_all(blocks, 'req', 0, 0, axis_index_groups=ROW_GROUPS, tiled=T...]
  transfers between devices with their start and end apart: 6 -> 6, of which waited for: 3 -> 2; matrix products, arithmetic and copies ran while one was open for 8% -> 7% of each run, Pallas kernels for 4% -> 4%
where the time goes in v2:
time: 165 us
  blocking collectives  50.1 us (30%)
  waiting for transfers between devices  29.7 us (18%)
  Pallas kernels  25.2 us (15%)
  starting transfers between devices  23.8 us (14%)
  between operations  17 us (10%)
  local copies, waits for them, and re-layouts  10.6 us (6%)
  other arithmetic  8.45 us (5%)
    all_to_all x1, blocking collectives, trade(): lax.all_to_all(blocks, 'req', 0, 0, axis_index_groups=ROW_GROUPS, tiled=T...  43.6 us
    all_to_all x1, waiting for transfers between devices, trade(): lax.all_to_all(blocks, 'req', 0, 0, axis_index_groups=ROW_GROUPS, tiled=T...  28.5 us
    ppermute x4, starting transfers between devices, swap(): return lax.ppermute(array, 'req', SWAP)  15.9 us
    pallas_call x1, Pallas kernels, visit(): pl.pallas_call(visit_kernel, out_shape=jax.ShapeDtypeStruct((sources, til...  10.4 us
    all_to_all x1, starting transfers between devices, trade(): lax.all_to_all(blocks, 'req', 0, 0, axis_index_groups=ROW_GROUPS, tiled=T...  7.96 us
    pallas_call x1, Pallas kernels, join(): pl.pallas_call(join_kernel, out_shape=jax.ShapeDtypeStruct((kv_heads, row...  7.55 us
    psum x1, blocking collectives, shards(): lax.psum(jnp.where(spot, meta, 0), ('req', 'head'), axis_index_groups=chips)  6.51 us
    pallas_call x1, Pallas kernels, suffix(): pl.pallas_call(suffix_kernel, out_shape=(jax.ShapeDtypeStruct((kv_heads,...  6.43 us
  transfers between devices with their start and end apart: 6, of which 2 were waited for; matrix products, arithmetic and copies ran while one was open for 7% of the time, Pallas kernels for 4%

profile of v2, /device:TPU:1, one launch (start us, length us, event | category | flops | bytes accessed | tf_op | source)
XLA Modules:
  0.0 164.8 jit_solution(4387545819159839770)
XLA Ops:
  6.5 1.2 reshape_squeeze.9
  7.8 1.2 broadcast_select_fusion.1
  9.1 8.8 %collective-permute-start.1 = (bf16[1024,128]{1,0:T(8,128)(2,1)S(1)}, bf16[1024,128]{1,0:T(8,128)(2,1)S(1)}, u32[]{:S(2)}, u32[]{:S(2)}) collective-permute-start(bf16[1024,128]{1,0:T(8,128)(2,1)S(1)} %bitcast.58), channel_id=1, source_target_pairs={{0,4},{4,0},{8,12},{12,8},{16,20},{20,16},{24,28},{28,24},{32,36},... | collective-permute-start | bytes 786440 | tf_op jit(solution)/shard_map/ppermute | solution.py:295
  18.0 6.5 %psum.7 = s32[8,2,16]{2,0,1:T(8,128)S(1)} all-reduce(s32[8,2,16]{2,0,1:T(8,128)S(1)} %broadcast_select_fusion.4), channel_id=1, replica_groups={{0,1,2,3,4,5,6,7},{8,9,10,11,12,13,14,15},{16,17,18,19,20,21,22,23},{24..., use_global_device_ids=true, to_apply=%region_0.1 | all-reduce | flops 256 | bytes 2048 | tf_op jit(solution)/shard_map/psum | solution.py:309
  24.5 0.9 pad_maximum_fusion.3
  25.4 0.7 reshape.286
  26.4 2.0 %collective-permute-start.2 = (bf16[64,32,128]{2,1,0:T(8,128)(2,1)S(1)}, bf16[64,32,128]{2,1,0:T(8,128)(2,1)S(1)}, u32[]{:S(2)}, u32[]{:S(2)}) collective-permute-start(bf16[64,32,128]{2,1,0:T(8,128)(2,1)S(1)} %get-tuple-element.130), channel_id=1, source_target_pairs={{0,4},{4,0},{8,12},{12,8},{16,20},{20,16},{24,28},{28,24},{32,36},... | collective-permute-start | bytes 1572872 | tf_op jit(solution)/shard_map/ppermute | solution.py:295
  29.2 0.6 fusion.3
  30.0 0.6 reduce_max.46
  30.6 0.6 reduce_max.47
  32.7 0.8 copy-done.9
  33.5 1.1 pad_maximum_fusion.2.query_ref
  34.6 0.9 send.3
  35.5 1.4 copy-done
  36.9 8.0 %all-to-all-start.2 = ((bf16[8,33,32,128]{3,2,1,0:T(8,128)(2,1)}), bf16[8,33,32,128]{3,2,1,0:T(8,128)(2,1)S(1)}, u32[]{:S(2)}, u32[]{:S(2)}) async-start(bf16[8,33,32,128]{3,2,1,0:T(8,128)(2,1)} %copy-done), calls=%async_computation.2 | async-start | bytes 4325376 | tf_op jit(solution)/shard_map/all_to_all | solution.py:360
  44.9 0.4 fusion.10
  45.5 1.8 %slice_bitcast_fusion = (bf16[64,32,256]{2,1,0:T(8,128)(2,1)S(1)}, bf16[64,32,256]{2,1,0:T(8,128)(2,1)S(1)}) fusion(bf16[64,2,32,256]{3,2,1,0:T(8,128)(2,1)} %param.11), kind=kLoop, calls=%fused_computation.19 | loop fusion | bytes 4194304 | tf_op jit(solution)/shard_map/squeeze | solution.py:367
  47.2 1.3 maximum_maximum_fusion.1
  48.5 6.4 %suffix.1 = (f32[2,64,32,128]{3,2,1,0:T(8,128)}, f32[2,64,32,128]{3,2,1,0:T(8,128)}, f32[2,64,32,128]{3,2,1,0:T(8,128)}) custom-call(s32[64]{0:T(128)S(1)} %fusion.6.length_ref, bf16[2,64,32,128]{3,2,1,0:T(8,128)(2,1)S(1)} %bitcast.52, bf16[64,48,256]{2,1,0:T(8,128)(2,1)S(1)} %get-tuple-element.138.key_ref, bf16[64,48,256]{2,1,0:T(8,128)(2,1)S(1)} %get-tuple-element.137.value_ref), custom_call_target="tpu_custom_call" | custom-call | flops 100663296 | bytes 8388608 | tf_op jit(solution)/shard_map/suffix/pallas_call | solution.py:230
  55.0 28.5 %all-to-all-done.2.query_ref = bf16[8,33,32,128]{3,2,1,0:T(8,128)(2,1)S(1)} async-done(((bf16[8,33,32,128]{3,2,1,0:T(8,128)(2,1)}), bf16[8,33,32,128]{3,2,1,0:T(8,128)(2,1)S(1)}, u32[]{:S(2)}, u32[]{:S(2)}) %all-to-all-start.2) | async-done | bytes 2162720 | tf_op jit(solution)/shard_map/all_to_all | solution.py:360
  83.5 0.7 slice_reduce_fusion.1
  84.2 0.7 broadcast_in_dim.125
  84.9 3.1 %collective-permute-start.3 = (f32[8,128]{1,0:T(8,128)S(1)}, f32[8,128]{1,0:T(8,128)S(1)}, u32[]{:S(2)}, u32[]{:S(2)}) collective-permute-start(f32[8,128]{1,0:T(8,128)S(1)} %broadcast_in_dim.125), channel_id=1, source_target_pairs={{0,4},{4,0},{8,12},{12,8},{16,20},{20,16},{24,28},{28,24},{32,36},... | collective-permute-start | bytes 12296 | tf_op jit(solution)/shard_map/ppermute | solution.py:295
  88.9 10.4 %visit.3 = bf16[8,34,32,128]{3,2,1,0:T(8,128)(2,1)S(1)} custom-call(f32[8,128]{1,0:T(8,128)S(1)} %broadcast_maximum_fusion.note_ref, bf16[8,33,32,128]{3,2,1,0:T(8,128)(2,1)S(1)} %all-to-all-done.2.query_ref, bf16[16,1024,128]{2,1,0:T(8,128)(2,1)} %all-gather.2.cloned.1.call-done.far_ref), custom_call_target="tpu_custom_call" | custom-call | tf_op jit(solution)/shard_map/visit/pallas_call | solution.py:166
  99.3 43.6 %all_to_all.20 = bf16[8,34,32,128]{3,2,1,0:T(8,128)(2,1)S(1)} all-to-all(bf16[8,34,32,128]{3,2,1,0:T(8,128)(2,1)S(1)} %visit.3), channel_id=1, replica_groups={{0,64,128,192,256,320,384,448},{8,72,136,200,264,328,392,456},{16,80,14..., dimensions={0} | all-to-all | bytes 4456448 | tf_op jit(solution)/shard_map/all_to_all | solution.py:360
  142.8 1.2 slice.68
  144.1 1.9 %collective-permute-start.4 = (bf16[8,17,32,128]{3,2,1,0:T(8,128)(2,1)}, bf16[8,17,32,128]{3,2,1,0:T(8,128)(2,1)}, u32[]{:S(2)}, u32[]{:S(2)}) collective-permute-start(bf16[8,17,32,128]{3,2,1,0:T(8,128)(2,1)} %slice.68), channel_id=1, source_target_pairs={{0,4},{4,0},{8,12},{12,8},{16,20},{20,16},{24,28},{28,24},{32,36},... | collective-permute-start | bytes 3342344 | tf_op jit(solution)/shard_map/ppermute | solution.py:295
  146.0 0.7 slice_reduce_fusion
  147.9 1.1 collective-permute-done.4
  149.0 7.5 %conditional.1 = (bf16[2,64,32,128]{3,2,1,0:T(8,128)(2,1)S(1)}) conditional(s32[]{:T(128)} %convert_element_type.40, (s32[2,64]{1,0:T(2,128)S(1)}, s32[2,64]{1,0:T(2,128)S(1)}, f32[]{:T(128)}, s32[2,64]{1,0:T(2,128)S(1)}, bf16[128,32,128]{2,1,0:T(8,128)(2,1)S(1)}, /*index=5*/f32[8,128]{1,0:T(8,128)S(1)}, bf16[16,1024,128]{2,1,0:T(8,128)(2,1)}, ...), branch_computations={%region_10.13_spmd, %region_13.14_spmd} | conditional | flops 3428880 | bytes 70802464 | solution.py:411
  149.0 7.5 %join.3 = bf16[2,64,32,128]{3,2,1,0:T(8,128)(2,1)S(1)} custom-call(s32[1]{0:T(128)} %get-tuple-element.64.core_ref, s32[384]{0:T(512)S(1)} %get-tuple-element.65.table_ref, bf16[272,32,128]{2,1,0:T(8,128)(2,1)S(1)} %get-tuple-element.66.mine_ref, bf16[136,32,128]{2,1,0:T(8,128)(2,1)} %get-tuple-element.67.theirs_ref, ...), custom_call_target="tpu_custom_call" | custom-call | tf_op jit(solution)/shard_map/cond/branch_1_fun/join/pallas_call | solution.py:277
  156.9 1.1 reshape.293
  (59 shorter events, 2.0 us)
Async XLA Ops:
  6.5 82.4 %all-gather.2.cloned.1.call-start = ((), (), s32[]{:S(2)}) async-start(), calls=%async_computation.4 | async-start | bytes 4718592 | tf_op jit(solution)/shard_map/all_gather | solution.py:311
  6.5 11.3 %copy-start.11 = (s32[16]{0:T(128)S(1)}, s32[16]{0:T(128)}, u32[]{:S(2)}) copy-start(s32[16]{0:T(128)} %param.14) | copy-start | bytes 196
  6.5 11.3 %copy-start.12 = (s32[16,1]{0,1:T(1,128)S(1)}, s32[16,1]{0,1:T(1,128)}, u32[]{:S(2)}) copy-start(s32[16,1]{0,1:T(1,128)} %param.13) | copy-start | bytes 196
  7.7 17.7 %copy-start.7 = (bf16[64,4,2048]{2,1,0:T(4,128)(2,1)S(1)}, bf16[64,4,2048]{2,1,0:T(4,128)(2,1)}, u32[]{:S(2)}) copy-start(bf16[64,4,2048]{2,1,0:T(4,128)(2,1)} %param.9) | copy-start | bytes 3145732
  9.1 15.4 %collective-permute-start.1 = (bf16[1024,128]{1,0:T(8,128)(2,1)S(1)}, bf16[1024,128]{1,0:T(8,128)(2,1)S(1)}, u32[]{:S(2)}, u32[]{:S(2)}) collective-permute-start(bf16[1024,128]{1,0:T(8,128)(2,1)S(1)} %bitcast.58), channel_id=1, source_target_pairs={{0,4},{4,0},{8,12},{12,8},{16,20},{20,16},{24,28},{28,24},{32,36},... | collective-permute-start | bytes 786440 | tf_op jit(solution)/shard_map/ppermute | solution.py:295
  26.1 2.5 %copy-start.10 = (s32[128]{0:T(128)S(1)}, s32[128]{0:T(128)}, u32[]{:S(2)}) copy-start(s32[128]{0:T(128)} %param.15) | copy-start | bytes 1540
  26.4 6.2 %collective-permute-start.2 = (bf16[64,32,128]{2,1,0:T(8,128)(2,1)S(1)}, bf16[64,32,128]{2,1,0:T(8,128)(2,1)S(1)}, u32[]{:S(2)}, u32[]{:S(2)}) collective-permute-start(bf16[64,32,128]{2,1,0:T(8,128)(2,1)S(1)} %get-tuple-element.130), channel_id=1, source_target_pairs={{0,4},{4,0},{8,12},{12,8},{16,20},{20,16},{24,28},{28,24},{32,36},... | collective-permute-start | bytes 1572872 | tf_op jit(solution)/shard_map/ppermute | solution.py:295
  32.7 0.8 copy-start.9
  34.6 2.3 %copy-start.2 = (bf16[128,32,128]{2,1,0:T(8,128)(2,1)}, bf16[128,32,128]{2,1,0:T(8,128)(2,1)S(1)}, u32[]{:S(2)}) copy-start(bf16[128,32,128]{2,1,0:T(8,128)(2,1)S(1)} %pad_maximum_fusion.2.query_ref) | copy-start | bytes 3145732
  35.5 1.4 copy-start
  36.9 8.1 %copy-start.8 = (bf16[64,4,2,256]{3,2,1,0:T(2,128)(2,1)S(1)}, bf16[64,4,2,256]{3,2,1,0:T(2,128)(2,1)}, u32[]{:S(2)}) copy-start(bf16[64,4,2,256]{3,2,1,0:T(2,128)(2,1)} %param.10) | copy-start | bytes 786436
  36.9 46.6 %all-to-all-start.2 = ((bf16[8,33,32,128]{3,2,1,0:T(8,128)(2,1)}), bf16[8,33,32,128]{3,2,1,0:T(8,128)(2,1)S(1)}, u32[]{:S(2)}, u32[]{:S(2)}) async-start(bf16[8,33,32,128]{3,2,1,0:T(8,128)(2,1)} %copy-done), calls=%async_computation.2 | async-start | bytes 4325376 | tf_op jit(solution)/shard_map/all_to_all | solution.py:360
  84.9 3.9 %collective-permute-start.3 = (f32[8,128]{1,0:T(8,128)S(1)}, f32[8,128]{1,0:T(8,128)S(1)}, u32[]{:S(2)}, u32[]{:S(2)}) collective-permute-start(f32[8,128]{1,0:T(8,128)S(1)} %broadcast_in_dim.125), channel_id=1, source_target_pairs={{0,4},{4,0},{8,12},{12,8},{16,20},{20,16},{24,28},{28,24},{32,36},... | collective-permute-start | bytes 12296 | tf_op jit(solution)/shard_map/ppermute | solution.py:295
  142.8 6.2 %copy-start.3 = (bf16[128,32,128]{2,1,0:T(8,128)(2,1)S(1)}, bf16[128,32,128]{2,1,0:T(8,128)(2,1)}, u32[]{:S(2)}) copy-start(bf16[128,32,128]{2,1,0:T(8,128)(2,1)} %copy-done.2) | copy-start | bytes 3145732
  144.1 5.0 %collective-permute-start.4 = (bf16[8,17,32,128]{3,2,1,0:T(8,128)(2,1)}, bf16[8,17,32,128]{3,2,1,0:T(8,128)(2,1)}, u32[]{:S(2)}, u32[]{:S(2)}) collective-permute-start(bf16[8,17,32,128]{3,2,1,0:T(8,128)(2,1)} %slice.68), channel_id=1, source_target_pairs={{0,4},{4,0},{8,12},{12,8},{16,20},{20,16},{24,28},{28,24},{32,36},... | collective-permute-start | bytes 3342344 | tf_op jit(solution)/shard_map/ppermute | solution.py:295
Sparse Core Ops, SparseCore 0:
  25.5 61.9 all-gather.1
